TPU v7x, 32 devices: a whole 2x2x4 slice. The times are simulated.
32 devices in a mesh: group: 4 (over x, core), dp: 2 (over y), tensor: 4 (over z).
Axes of the slice: x: 2, y: 2, z: 4, core: 2. Of those that a mesh axis runs over, the one named last changes fastest.
Arguments:
- keyvalue_local: float32 [4, 2, 4096, 1024], P('group', None, 'dp', 'tensor'), may hold values from -6 to 6
- keyvalue_anchor: float32 [2, 4096, 1024], P(None, 'dp', 'tensor'), may hold values from -6 to 6
- keyvalue_state: float32 [2, 4096, 1024], P(None, 'dp', 'tensor'), may hold values from -6 to 6
- router_local: float32 [4, 4096, 8], P('group', 'dp'), may hold values from -6 to 6
- router_anchor: float32 [4096, 8], P('dp'), may hold values from -6 to 6
- router_state: float32 [4096, 8], P('dp'), may hold values from -6 to 6
- gain_local: float32 [4, 2, 4096], P('group', None, 'dp'), may hold values from -6 to 6
- gain_anchor: float32 [2, 4096], P(None, 'dp'), may hold values from -6 to 6
- gain_state: float32 [2, 4096], P(None, 'dp'), may hold values from -6 to 6
- embed_local: float32 [4, 250, 4096], P('group', 'dp', 'tensor'), may hold values from -6 to 6
- embed_anchor: float32 [250, 4096], P('dp', 'tensor'), may hold values from -6 to 6
- embed_state: float32 [250, 4096], P('dp', 'tensor'), may hold values from -6 to 6
- embed_basis: float32 [4096, 64], P('tensor'), may hold values from -0.25 to 0.25
- outer_rate: float32 [], replicated, may hold values from 0.5 to 1
Outputs:
- keyvalue_average: float32 [2, 4096, 1024], P(None, 'dp', 'tensor')
- keyvalue_momentum: float32 [2, 4096, 1024], P(None, 'dp', 'tensor')
- keyvalue_updated: float32 [2, 4096, 1024], P(None, 'dp', 'tensor')
- router_average: float32 [4096, 8], P('dp')
- router_momentum: float32 [4096, 8], P('dp')
- router_updated: float32 [4096, 8], P('dp')
- gain_average: float32 [2, 4096], P(None, 'dp')
- gain_momentum: float32 [2, 4096], P(None, 'dp')
- gain_updated: float32 [2, 4096], P(None, 'dp')
- embed_average: float32 [250, 4096], P('dp', 'tensor')
- embed_momentum: float32 [250, 4096], P('dp', 'tensor')
- embed_updated: float32 [250, 4096], P('dp', 'tensor')
All inputs are finite; a program needn't handle non-finite values.
Results may differ from a plain program's by a relative error of at most 0.0001.
Values sent between devices are 32-bit elements; how exact they have to be, the bound alone decides.
A program may use at most 128 MiB of HBM per device.

v0:
```python
import jax
import jax.numpy as jnp
from jax import lax
from jax.sharding import PartitionSpec as P


def nesterov(average, state, anchor, outer_rate):
    momentum = 0.5 * state + average
    updated = anchor - outer_rate * (average + 0.5 * momentum)
    return (average, momentum, updated)


def owned_slice(whole, position, count, axis_dim):
    return lax.dynamic_slice_in_dim(whole, position * count, count, axis_dim)


def local(
    keyvalue_local,
    keyvalue_anchor,
    keyvalue_state,
    router_local,
    router_anchor,
    router_state,
    gain_local,
    gain_anchor,
    gain_state,
    embed_local,
    embed_anchor,
    embed_state,
    embed_basis,
    outer_rate,
):
    groups = lax.axis_size("group")
    keyvalue_diff = keyvalue_anchor - keyvalue_local[0]
    router_diff = router_anchor - router_local[0]
    gain_diff = gain_anchor - gain_local[0]
    keyvalue_sum, router_sum, gain_sum = (
        lax.psum_scatter(keyvalue_diff, "group", scatter_dimension=1, tiled=True),
        lax.psum_scatter(router_diff, "group", scatter_dimension=0, tiled=True),
        lax.psum_scatter(gain_diff, "group", scatter_dimension=1, tiled=True),
    )
    position = lax.axis_index("group")
    keyvalue_rows = keyvalue_anchor.shape[1] // groups
    router_rows = router_anchor.shape[0] // groups
    gain_rows = gain_anchor.shape[1] // groups
    keyvalue_part = nesterov(
        keyvalue_sum / groups,
        owned_slice(keyvalue_state, position, keyvalue_rows, 1),
        owned_slice(keyvalue_anchor, position, keyvalue_rows, 1),
        outer_rate,
    )
    router_part = nesterov(
        router_sum / groups,
        owned_slice(router_state, position, router_rows, 0),
        owned_slice(router_anchor, position, router_rows, 0),
        outer_rate,
    )
    gain_part = nesterov(
        gain_sum / groups,
        owned_slice(gain_state, position, gain_rows, 1),
        owned_slice(gain_anchor, position, gain_rows, 1),
        outer_rate,
    )
    gathered = (
        lax.all_gather(keyvalue_part[0], "group", axis=1, tiled=True),
        lax.all_gather(keyvalue_part[1], "group", axis=1, tiled=True),
        lax.all_gather(keyvalue_part[2], "group", axis=1, tiled=True),
        lax.all_gather(router_part[0], "group", axis=0, tiled=True),
        lax.all_gather(router_part[1], "group", axis=0, tiled=True),
        lax.all_gather(router_part[2], "group", axis=0, tiled=True),
        lax.all_gather(gain_part[0], "group", axis=1, tiled=True),
        lax.all_gather(gain_part[1], "group", axis=1, tiled=True),
        lax.all_gather(gain_part[2], "group", axis=1, tiled=True),
    )
    keyvalue_out = gathered[0:3]
    router_out = gathered[3:6]
    gain_out = gathered[6:9]
    partial_factors = jnp.dot(
        embed_anchor - embed_local[0],
        embed_basis,
        precision=lax.Precision.HIGHEST,
        preferred_element_type=jnp.float32,
    )
    factors = lax.psum(partial_factors, ("group", "tensor"))
    factors = factors / groups
    embed_average = jnp.dot(
        factors, embed_basis.T, precision=lax.Precision.HIGHEST, preferred_element_type=jnp.float32
    )
    embed_out = nesterov(embed_average, embed_state, embed_anchor, outer_rate)
    return (
        keyvalue_out[0],
        keyvalue_out[1],
        keyvalue_out[2],
        router_out[0],
        router_out[1],
        router_out[2],
        gain_out[0],
        gain_out[1],
        gain_out[2],
        embed_out[0],
        embed_out[1],
        embed_out[2],
    )


def solution(mesh):
    in_specs = (
        P("group", None, "dp", "tensor"),
        P(None, "dp", "tensor"),
        P(None, "dp", "tensor"),
        P("group", "dp", None),
        P("dp", None),
        P("dp", None),
        P("group", None, "dp"),
        P(None, "dp"),
        P(None, "dp"),
        P("group", "dp", "tensor"),
        P("dp", "tensor"),
        P("dp", "tensor"),
        P("tensor", None),
        P(),
    )
    out_specs = (
        P(None, "dp", "tensor"),
        P(None, "dp", "tensor"),
        P(None, "dp", "tensor"),
        P("dp", None),
        P("dp", None),
        P("dp", None),
        P(None, "dp"),
        P(None, "dp"),
        P(None, "dp"),
        P("dp", "tensor"),
        P("dp", "tensor"),
        P("dp", "tensor"),
    )
    return jax.shard_map(local, mesh=mesh, in_specs=in_specs, out_specs=out_specs, check_vma=False)
```

profile of v0, /device:TPU:0, one launch (start us, length us, event | category | flops | bytes accessed | tf_op | source)
XLA Modules:
  0.0 241.7 jit_solution(5853017233001308531)
XLA Ops:
  7.2 6.0 %bitcast_subtract_fusion = f32[2,2048,256]{2,1,0:T(8,128)} fusion(f32[2,2048,256]{2,1,0:T(8,128)} %param.15, f32[1,2,2048,256]{3,2,1,0:T(8,128)} %param.14), kind=kLoop, calls=%fused_computation | loop fusion | flops 1048576 | bytes 12582912 | tf_op jit(solution)/shard_map/sub | solution.py:34
  13.4 0.6 copy-done.8
  14.0 1.4 copy.26
  15.5 0.6 bitcast_subtract_fusion.3
  16.9 43.7 %reduce-scatter.6.cloned.1.call-done = f32[2,512,256]{2,1,0:T(8,128)} async-done(((f32[2,2048,256]{2,1,0:T(8,128)}), f32[2,512,256]{2,1,0:T(8,128)}) %reduce-scatter.6.cloned.1.call-update) | async-done | bytes 1048592 | tf_op jit(solution)/shard_map/reduce_scatter | solution.py:38
  60.7 3.8 %multiply_subtract_fusion = (f32[2,512,256]{2,1,0:T(8,128)}, f32[2,512,256]{2,1,0:T(8,128)}, f32[2,512,256]{2,1,0:T(8,128)}) fusion(f32[2,2048,256]{2,1,0:T(8,128)} %param.15, s32[]{:T(128)S(6)} %select_n.2, f32[]{:T(128)S(6)} %copy.42, f32[2,512,256]{2,1,0:T(8,128)} %reduce-scatter.6.cloned.1.call-done, f32[2,2048,256]{2,1,0:T(8,128)} %param.16), kind=kLoop, calls=%fused_computation.1 | loop fusion | flops 1835008 | bytes 6291464 | tf_op jit(solution)/shard_map/sub | solution.py:9
  64.5 0.5 all-gather.6.cloned.1.call-update
  65.1 0.5 all-gather.8.cloned.1.call-update
  65.7 0.6 fusion
  66.3 60.9 %psum.7 = f32[125,64]{1,0:T(8,128)S(1)} all-reduce(f32[125,64]{1,0:T(8,128)S(1)} %fusion), channel_id=1, replica_groups=mesh['group'=4,'dp'=2,'tensor'=4] {'group','tensor'}, use_global_device_ids=true, to_apply=%region_3.0 | all-reduce | flops 8000 | bytes 64000 | tf_op jit(solution)/shard_map/psum | solution.py:84
  127.2 1.8 multiply_subtract_fusion.1
  129.0 1.1 copy.27
  130.0 0.7 multiply_subtract_fusion.3
  130.8 5.2 %all_gather.33 = f32[2,2048]{1,0:T(2,128)S(1)} all-gather(f32[2,512]{1,0:T(2,128)S(1)} %get-tuple-element.22), channel_id=1, replica_groups=mesh['group'=4,'dp'=2,'tensor'=4] {'group'}, dimensions={1}, use_global_device_ids=true | all-gather | bytes 20480 | tf_op jit(solution)/shard_map/all_gather | solution.py:71
  136.0 5.2 %all_gather.34 = f32[2,2048]{1,0:T(2,128)S(1)} all-gather(f32[2,512]{1,0:T(2,128)S(1)} %get-tuple-element.20), channel_id=1, replica_groups=mesh['group'=4,'dp'=2,'tensor'=4] {'group'}, dimensions={1}, use_global_device_ids=true | all-gather | bytes 20480 | tf_op jit(solution)/shard_map/all_gather | solution.py:72
  141.2 5.2 %all_gather.35 = f32[2,2048]{1,0:T(2,128)S(1)} all-gather(f32[2,512]{1,0:T(2,128)S(1)} %get-tuple-element.19), channel_id=1, replica_groups=mesh['group'=4,'dp'=2,'tensor'=4] {'group'}, dimensions={1}, use_global_device_ids=true | all-gather | bytes 20480 | tf_op jit(solution)/shard_map/all_gather | solution.py:73
  146.4 0.7 multiply_subtract_fusion.2
  147.2 5.2 %all_gather.30 = f32[2048,8]{0,1:T(8,128)S(1)} all-gather(f32[512,8]{0,1:T(8,128)S(1)} %get-tuple-element.21), channel_id=1, replica_groups=mesh['group'=4,'dp'=2,'tensor'=4] {'group'}, dimensions={0}, use_global_device_ids=true | all-gather | bytes 81920 | tf_op jit(solution)/shard_map/all_gather | solution.py:68
  152.4 5.2 %all_gather.31 = f32[2048,8]{0,1:T(8,128)S(1)} all-gather(f32[512,8]{0,1:T(8,128)S(1)} %get-tuple-element.18), channel_id=1, replica_groups=mesh['group'=4,'dp'=2,'tensor'=4] {'group'}, dimensions={0}, use_global_device_ids=true | all-gather | bytes 81920 | tf_op jit(solution)/shard_map/all_gather | solution.py:69
  157.6 5.5 %all_gather.32 = f32[2048,8]{0,1:T(8,128)S(1)} all-gather(f32[512,8]{0,1:T(8,128)S(1)} %get-tuple-element.17), channel_id=1, replica_groups=mesh['group'=4,'dp'=2,'tensor'=4] {'group'}, dimensions={0}, use_global_device_ids=true | all-gather | bytes 81920 | tf_op jit(solution)/shard_map/all_gather | solution.py:70
  163.1 21.5 %all-gather.6.cloned.1.call-done = f32[2,2048,256]{2,1,0:T(8,128)} async-done(((f32[2,512,256]{2,1,0:T(8,128)}), f32[2,2048,256]{2,1,0:T(8,128)}) %all-gather.6.cloned.1.call-update) | async-done | bytes 4194320 | tf_op jit(solution)/shard_map/all_gather | solution.py:66
  184.6 36.2 %all-gather.8.cloned.1.call-done = f32[2,2048,256]{2,1,0:T(8,128)} async-done(((f32[2,512,256]{2,1,0:T(8,128)}), f32[2,2048,256]{2,1,0:T(8,128)}) %all-gather.8.cloned.1.call-update) | async-done | bytes 4194320 | tf_op jit(solution)/shard_map/all_gather | solution.py:67
  220.8 4.6 %copy.43 = f32[2,2048,256]{2,1,0:T(8,128)} copy(f32[2,2048,256]{2,1,0:T(8,128)} %all-gather.4.cloned.1.call-done) | data formatting | bytes 8388608
  225.5 2.1 copy.44
  227.6 1.6 copy-done.2
  229.2 2.0 copy.45
  231.2 0.6 copy.46
  231.8 0.6 copy.47
  232.5 0.6 copy.48
  233.1 0.6 copy.49
  233.7 0.6 copy.50
  234.3 0.6 copy.51
  (32 shorter events, 0.4 us)
Async XLA Ops:
  7.2 58.5 %copy-start = (f32[1024,64]{0,1:T(8,128)S(1)}, f32[1024,64]{0,1:T(8,128)}, u32[]{:S(2)}) copy-start(f32[1024,64]{0,1:T(8,128)} %param.26) | copy-start | bytes 786436
  7.2 53.5 %reduce-scatter.6.cloned.1.call-start = ((), (), s32[]{:S(2)}) async-start(), calls=%async_computation.3 | async-start | bytes 5242880 | tf_op jit(solution)/shard_map/reduce_scatter | solution.py:38
  13.3 0.7 copy-start.8
  13.3 0.7 copy-start.9
  13.3 2.2 copy-start.6
  13.3 2.2 copy-start.7
  13.3 115.7 %reduce-scatter.10.cloned.1.call-start = ((), (), s32[]{:S(2)}) async-start(), calls=%async_computation.8 | async-start | bytes 1310720
  15.5 131.0 %reduce-scatter.8.cloned.1.call-start = ((), (), s32[]{:S(2)}) async-start(), calls=%async_computation.7 | async-start | bytes 81920 | tf_op jit(solution)/shard_map/reduce_scatter | solution.py:39
  16.2 146.9 %all-gather.4.cloned.1.call-start = ((), (), s32[]{:S(2)}) async-start(), calls=%async_computation.4 | async-start | bytes 5242880 | tf_op jit(solution)/shard_map/all_gather | solution.py:65
  16.9 48.8 %copy-start.3 = (f32[125,1024]{1,0:T(8,128)S(1)}, f32[125,1024]{1,0:T(8,128)}, u32[]{:S(2)}) copy-start(f32[125,1024]{1,0:T(8,128)} %param.24) | copy-start | bytes 1536004
  16.9 48.8 %copy-start.4 = (f32[1,125,1024]{2,0,1:T(1,128)S(1)}, f32[1,125,1024]{2,0,1:T(1,128)}, u32[]{:S(2)}) copy-start(f32[1,125,1024]{2,0,1:T(1,128)} %param.23) | copy-start | bytes 1536004
  16.9 110.3 %copy-start.5 = (f32[125,1024]{1,0:T(8,128)S(1)}, f32[125,1024]{1,0:T(8,128)}, u32[]{:S(2)}) copy-start(f32[125,1024]{1,0:T(8,128)} %param.25) | copy-start | bytes 1536004
  64.5 120.1 %all-gather.6.cloned.1.call-start = ((), (), s32[]{:S(2)}) async-start(), calls=%async_computation.5 | async-start | bytes 5242880 | tf_op jit(solution)/shard_map/all_gather | solution.py:66
  65.1 155.8 %all-gather.8.cloned.1.call-start = ((), (), s32[]{:S(2)}) async-start(), calls=%async_computation.6 | async-start | bytes 5242880 | tf_op jit(solution)/shard_map/all_gather | solution.py:67
  220.8 4.6 %copy-start.1 = (f32[2,2048,256]{2,1,0:T(8,128)S(1)}, f32[2,2048,256]{2,1,0:T(8,128)}, u32[]{:S(2)}) copy-start(f32[2,2048,256]{2,1,0:T(8,128)} %all-gather.6.cloned.1.call-done) | copy-start | bytes 12582916
  225.5 3.7 %copy-start.2 = (f32[2,2048,256]{2,1,0:T(8,128)S(1)}, f32[2,2048,256]{2,1,0:T(8,128)}, u32[]{:S(2)}) copy-start(f32[2,2048,256]{2,1,0:T(8,128)} %all-gather.8.cloned.1.call-done) | copy-start | bytes 12582916
Sparse Core Ops, SparseCore 0:
  13.4 47.1 reduce-scatter.5
  63.4 24.9 reduce-scatter.9
  91.3 19.4 reduce-scatter.7
  112.9 34.7 all-gather.3
  149.8 34.7 all-gather.5
  186.7 34.1 all-gather.7
where the time goes:
time: 242 us
  waiting for transfers between devices  103 us (43%)
  blocking collectives  92.5 us (38%)
  local copies, waits for them, and re-layouts  17.2 us (7%)
  between operations  14.9 us (6%)
  other arithmetic  11.9 us (5%)
    psum x1, blocking collectives, local(): factors = lax.psum(partial_factors, ('group', 'tensor'))  60.9 us
    reduce_scatter x1, waiting for transfers between devices, local(): lax.psum_scatter(keyvalue_diff, 'group', scatter_dimension=1, tiled=True)  43.7 us
    all_gather x1, waiting for transfers between devices, local(): lax.all_gather(keyvalue_part[2], 'group', axis=1, tiled=True)  36.2 us
    all_gather x1, waiting for transfers between devices, local(): lax.all_gather(keyvalue_part[1], 'group', axis=1, tiled=True)  21.5 us
    unnamed x31, local copies, waits for them, and re-layouts  17.2 us
    sub x1, other arithmetic, local(): keyvalue_diff = keyvalue_anchor - keyvalue_local[0]  6.04 us
    all_gather x1, blocking collectives, local(): lax.all_gather(router_part[2], 'group', axis=0, tiled=True)  5.46 us
    all_gather x1, blocking collectives, local(): lax.all_gather(router_part[0], 'group', axis=0, tiled=True)  5.25 us
  transfers between devices with their start and end apart: 6, of which 3 were waited for; matrix products, arithmetic and copies ran while one was open for 4% of the time, Pallas kernels for 0%

commit v1 on v0

v1 whole, which is shorter than its diff:
```python
import functools

import jax
import jax.numpy as jnp
from jax import lax
from jax.experimental import pallas as pl
from jax.experimental.pallas import tpu as pltpu
from jax.sharding import PartitionSpec as P

MESH = pl.DeviceIdType.MESH


def nesterov(average, state, anchor, rate):
    momentum = 0.5 * state + average
    return momentum, anchor - rate * (average + 0.5 * momentum)


def mean(total, groups):
    if groups & (groups - 1) == 0:
        return total * (1.0 / groups)
    return total / float(groups)


def exchange_kernel(
    chips, tensors, chunks, vocab,
    rate_ref, kl, ka, ks, rl, ra, rs, gl, ga, gs, el, ea, es, eb,
    k_avg, k_mom, k_upd, r_avg, r_mom, r_upd, g_avg, g_mom, g_upd, e_avg, e_mom, e_upd,
    a_v, l_v, s_v, pair_v, x_v,
    rl_v, ra_v, rs_v, gl_v, ga_v, gs_v, el_v, ea_v, es_v, eb_v, ed_v,
    r_d, r_pair, r_x, r_a, g_d, g_pair, g_x, g_a, f_d, f_pair, f_x, f_z, f_a,
    a_sem, l_sem, s_sem, small_sem,
    d_send, d_recv, x_send, x_recv, c_send, c_recv,
    sd_send, sd_recv, sx_send, sx_recv, sc_send, sc_recv, z_send, z_recv,
):
    groups = 2 * chips
    me = lax.axis_index("group")
    chip, core = me // 2, lax.rem(me, 2)
    other = 1 - core
    sibling = chip * 2 + other
    lane = lax.axis_index("tensor")
    rows = a_v.shape[1] // chunks
    half_rows = a_v.shape[1]

    def load(src, dst, sem, half, c):
        at = pl.multiple_of(c * rows, rows)
        return pltpu.make_async_copy(
            src.at[half, pl.ds(at, rows), :], dst.at[half, pl.ds(at, rows), :], sem.at[half, c]
        )

    def start_loads(c, _):
        for half in (other, core):
            load(ka, a_v, a_sem, half, c).start()
            load(kl, l_v, l_sem, half, c).start()
        return 0

    small_loads = [
        pltpu.make_async_copy(src, dst, small_sem.at[i])
        for i, (src, dst) in enumerate(
            [(ea, ea_v), (el, el_v), (eb, eb_v), (rl, rl_v), (ra, ra_v), (gl, gl_v), (ga, ga_v),
             (rs, rs_v), (gs, gs_v), (es, es_v)]
        )
    ]
    lead = min(4, chunks)
    lax.fori_loop(0, lead, start_loads, 0)
    for copy in small_loads[:7]:
        copy.start()

    barrier = pltpu.get_barrier_semaphore()
    pl.semaphore_signal(barrier, inc=1, device_id={"group": sibling}, device_id_type=MESH)
    for j in range(1, chips):
        peer = lax.rem(chip + j, chips) * 2 + core
        pl.semaphore_signal(barrier, inc=1, device_id={"group": peer}, device_id_type=MESH)
    for j in range(1, tensors):
        peer = lax.rem(lane + j, tensors)
        pl.semaphore_signal(barrier, inc=1, device_id={"tensor": peer}, device_id_type=MESH)

    lax.fori_loop(lead, chunks, start_loads, 0)
    for copy in small_loads[7:]:
        copy.start()
    s_loads = [
        pltpu.make_async_copy(ks.at[half], s_v.at[half], s_sem.at[half]) for half in (0, 1)
    ]
    for copy in s_loads:
        copy.start()
    pl.semaphore_wait(barrier, chips + tensors - 1)

    def to_sibling(src, dst, send, recv):
        return pltpu.make_async_remote_copy(
            src_ref=src, dst_ref=dst, send_sem=send, recv_sem=recv,
            device_id={"group": sibling}, device_id_type=MESH,
        )

    def to_chip(j, src, dst, send, recv):
        return pltpu.make_async_remote_copy(
            src_ref=src, dst_ref=dst, send_sem=send, recv_sem=recv,
            device_id={"group": lax.rem(chip + j, chips) * 2 + core}, device_id_type=MESH,
        )

    def part(c):
        return pl.ds(pl.multiple_of(c * rows, rows), rows)

    def pair_copy(c):
        return to_sibling(l_v.at[other, part(c), :], pair_v.at[part(c), :], d_send.at[c], d_recv.at[c])

    def chip_copy(c, j, source):
        return to_chip(
            j, x_v.at[source, part(c), :], x_v.at[source, part(c), :],
            x_send.at[j - 1, c], x_recv.at[source, c],
        )

    def share_copy(c, half):
        return to_sibling(k_avg.at[half, part(c), :], k_avg.at[half, part(c), :], c_send.at[c], c_recv.at[c])

    def give(c):
        load(ka, a_v, a_sem, other, c).wait()
        load(kl, l_v, l_sem, other, c).wait()
        l_v[other, part(c), :] = a_v[other, part(c), :] - l_v[other, part(c), :]
        pair_copy(c).start()
        load(ka, a_v, a_sem, core, c).wait()
        load(kl, l_v, l_sem, core, c).wait()

    def send(c):
        copy = pair_copy(c)
        copy.wait_recv()
        x_v[chip, part(c), :] = (
            a_v[core, part(c), :] - l_v[core, part(c), :]
        ) + pair_v[part(c), :]
        for j in range(1, chips):
            chip_copy(c, j, chip).start()

    def give_and_send(c, _):
        give(c)
        send(c - 1)
        return 0

    give(0)
    lax.fori_loop(1, lead, give_and_send, 0)

    for copy in small_loads[:7]:
        copy.wait()
    smalls = [(r_d, r_pair, r_x, r_a), (g_d, g_pair, g_x, g_a), (f_d, f_pair, f_x, f_a)]

    ed_v[...] = jnp.zeros_like(ed_v)
    blocks = el_v.shape[1]
    for b in range(blocks):
        ed_v[0:vocab, b * 128 : (b + 1) * 128] = ea_v[:, b * 128 : (b + 1) * 128] - el_v[:, b, :]
    r_half = r_d.shape[2]
    g_half = g_d.shape[2]
    for h in (0, 1):
        r_d[h] = ra_v[:, h * r_half : (h + 1) * r_half] - rl_v[:, h * r_half : (h + 1) * r_half]
        g_d[h] = ga_v[:, h * g_half : (h + 1) * g_half] - gl_v[:, h * g_half : (h + 1) * g_half]
    factors = lax.dot_general(
        eb_v[...], ed_v[...], (((1,), (1,)), ((), ())),
        precision=lax.Precision.HIGHEST, preferred_element_type=jnp.float32,
    )
    rank_half = f_d.shape[1]
    for h in (0, 1):
        f_d[h] = factors[h * rank_half : (h + 1) * rank_half, :]
    small_pair = [
        to_sibling(d.at[other], pair, sd_send.at[i], sd_recv.at[i])
        for i, (d, pair, x, a) in enumerate(smalls)
    ]
    for copy in small_pair:
        copy.start()
    for i, (d, pair, x, a) in enumerate(smalls):
        small_pair[i].wait_recv()
        x[chip] = d[core] + pair[...]
        for j in range(1, chips):
            to_chip(j, x.at[chip], x.at[chip], sx_send.at[i, j - 1], sx_recv.at[i, chip]).start()

    lax.fori_loop(lead, chunks, give_and_send, 0)
    send(chunks - 1)
    for copy in s_loads + small_loads[7:]:
        copy.wait()

    rate = rate_ref[0]

    def gather(c):
        for j in range(1, chips):
            chip_copy(c, j, lax.rem(chip + j, chips)).wait_recv()
        total = x_v[0, part(c), :]
        for q in range(1, chips):
            total = total + x_v[q, part(c), :]
        average = mean(total, groups)
        k_avg[core, part(c), :] = average
        share_copy(c, core).start()
        momentum, updated = nesterov(average, s_v[core, part(c), :], a_v[core, part(c), :], rate)
        k_mom[core, part(c), :] = momentum
        k_upd[core, part(c), :] = updated

    def accept(c):
        share_copy(c, other).wait_recv()
        momentum, updated = nesterov(
            k_avg[other, part(c), :], s_v[other, part(c), :], a_v[other, part(c), :], rate
        )
        k_mom[other, part(c), :] = momentum
        k_upd[other, part(c), :] = updated

    def gather_and_accept(c, _):
        gather(c)
        accept(c - 1)
        return 0

    cut1 = max(lead, chunks // 2)
    cut2 = max(cut1, (3 * chunks) // 4)
    cut3 = max(cut2, (7 * chunks) // 8)
    gather(0)
    lax.fori_loop(1, cut1, gather_and_accept, 0)

    def small_share(i, half):
        a = smalls[i][3]
        return to_sibling(a.at[half], a.at[half], sc_send.at[i], sc_recv.at[i])

    def z_copy(j, source):
        return pltpu.make_async_remote_copy(
            src_ref=f_z.at[source], dst_ref=f_z.at[source], send_sem=z_send.at[j - 1],
            recv_sem=z_recv.at[source], device_id={"tensor": lax.rem(lane + j, tensors)},
            device_id_type=MESH,
        )

    for i, (d, pair, x, a) in enumerate(smalls):
        for j in range(1, chips):
            q = lax.rem(chip + j, chips)
            to_chip(j, x.at[q], x.at[q], sx_send.at[i, j - 1], sx_recv.at[i, q]).wait_recv()
        total = x[0]
        for q in range(1, chips):
            total = total + x[q]
        if i < 2:
            a[core] = mean(total, groups)
            small_share(i, core).start()
        else:
            f_z[lane] = total
            for j in range(1, tensors):
                z_copy(j, lane).start()

    lax.fori_loop(cut1, cut2, gather_and_accept, 0)

    for j in range(1, tensors):
        z_copy(j, lax.rem(lane + j, tensors)).wait_recv()
    total = f_z[0]
    for t in range(1, tensors):
        total = total + f_z[t]
    f_a[core] = mean(total, groups)
    small_share(2, core).start()
    for i, half, avg, mom, upd, a, st, an in (
        (0, r_half, r_avg, r_mom, r_upd, r_a, rs_v, ra_v),
        (1, g_half, g_avg, g_mom, g_upd, g_a, gs_v, ga_v),
    ):
        small_share(i, other).wait_recv()
        for h in (0, 1):
            at = slice(h * half, (h + 1) * half)
            average = a[h]
            momentum, updated = nesterov(average, st[:, at], an[:, at], rate)
            avg[:, at] = average
            mom[:, at] = momentum
            upd[:, at] = updated

    lax.fori_loop(cut2, cut3, gather_and_accept, 0)

    small_share(2, other).wait_recv()
    turned = jnp.concatenate([f_a[0], f_a[1]], axis=0).T
    average = lax.dot_general(
        turned, eb_v[...], (((1,), (0,)), ((), ())),
        precision=lax.Precision.HIGHEST, preferred_element_type=jnp.float32,
    )[0:vocab, :]
    momentum, updated = nesterov(average, es_v[...], ea_v[...], rate)
    e_avg[...] = average
    e_mom[...] = momentum
    e_upd[...] = updated

    lax.fori_loop(cut3, chunks, gather_and_accept, 0)
    accept(chunks - 1)

    def drain(c, _):
        pair_copy(c).wait_send()
        for j in range(1, chips):
            chip_copy(c, j, chip).wait_send()
        share_copy(c, core).wait_send()
        return 0

    lax.fori_loop(0, chunks, drain, 0)
    for i, (d, pair, x, a) in enumerate(smalls):
        small_pair[i].wait_send()
        for j in range(1, chips):
            to_chip(j, x.at[chip], x.at[chip], sx_send.at[i, j - 1], sx_recv.at[i, chip]).wait_send()
        small_share(i, core).wait_send()
    for j in range(1, tensors):
        z_copy(j, lane).wait_send()


def store_kernel(count, *refs):
    sem = refs[-1]
    copies = [
        pltpu.make_async_copy(refs[i], refs[count + i], sem.at[i]) for i in range(count)
    ]
    for copy in copies:
        copy.start()
    for copy in copies:
        copy.wait()


def local(groups, tensors, kl, ka, ks, rl, ra, rs, gl, ga, gs, el, ea, es, eb, rate):
    chips = groups // 2
    f32 = jnp.float32
    rows, width = ka.shape[0] * ka.shape[1] // 2, ka.shape[2]
    chunks = 16
    while rows % (8 * chunks):
        chunks //= 2
    vocab, columns = ea.shape
    rank = eb.shape[1]
    padded = -(-vocab // 128) * 128
    blocks = columns // 128
    router_rows, experts = ra.shape
    gains, gain_rows = ga.shape
    operands = (
        rate.reshape(1),
        kl.reshape(2, rows, width), ka.reshape(2, rows, width), ks.reshape(2, rows, width),
        rl[0].T, ra.T, rs.T,
        gl[0], ga, gs,
        el.reshape(vocab, blocks, 128), ea, es, eb.T,
    )
    kv_shape, r_shape, g_shape, e_shape = (
        (2, rows, width), (experts, router_rows), (gains, gain_rows), (vocab, columns)
    )
    shapes = [s for s in (kv_shape, r_shape, g_shape, e_shape) for _ in range(3)]
    r_part, g_part, f_part = (
        (experts, router_rows // 2), (gains, gain_rows // 2), (rank // 2, padded)
    )
    vmem = lambda *s: pltpu.VMEM(s, f32)
    dma = lambda *s: pltpu.SemaphoreType.DMA(s)

    def sums(part, slots):
        return [vmem(2, *part), vmem(*part), vmem(chips, *part)] + slots + [vmem(2, *part)]

    scratch = [
        vmem(*kv_shape), vmem(*kv_shape), vmem(*kv_shape), vmem(rows, width), vmem(chips, rows, width),
        vmem(*r_shape), vmem(*r_shape), vmem(*r_shape),
        vmem(*g_shape), vmem(*g_shape), vmem(*g_shape),
        vmem(vocab, blocks, 128), vmem(*e_shape), vmem(*e_shape), vmem(rank, columns),
        vmem(padded, columns),
    ]
    scratch += sums(r_part, []) + sums(g_part, []) + sums(f_part, [vmem(tensors, *f_part)])
    peers = max(chips - 1, 1)
    scratch += [
        dma(2, chunks), dma(2, chunks), dma(2), dma(10),
        dma(chunks), dma(chunks), dma(peers, chunks), dma(chips, chunks), dma(chunks), dma(chunks),
        dma(3), dma(3), dma(3, peers), dma(3, chips), dma(3), dma(3),
        dma(max(tensors - 1, 1)), dma(tensors),
    ]
    hold = pl.pallas_call(
        functools.partial(exchange_kernel, chips, tensors, chunks, vocab),
        out_shape=[pltpu.VMEM(s, f32) for s in shapes],
        in_specs=[pl.BlockSpec(memory_space=pltpu.SMEM)] + [pl.BlockSpec(memory_space=pl.ANY)] * 13,
        out_specs=[pl.BlockSpec(memory_space=pltpu.VMEM)] * 12,
        scratch_shapes=scratch,
        compiler_params=pltpu.CompilerParams(
            collective_id=0, has_side_effects=True, vmem_limit_bytes=40 * 2**20
        ),
        name="exchange",
    )(*operands)
    out = pl.pallas_call(
        functools.partial(store_kernel, 12),
        out_shape=[jax.ShapeDtypeStruct(s, f32) for s in shapes],
        in_specs=[pl.BlockSpec(memory_space=pltpu.VMEM)] * 12,
        out_specs=[pl.BlockSpec(memory_space=pl.ANY)] * 12,
        scratch_shapes=[dma(12)],
        compiler_params=pltpu.CompilerParams(vmem_limit_bytes=20 * 2**20),
        name="store",
    )(*hold)
    return (
        *(o.reshape(ka.shape) for o in out[0:3]),
        *(o.T for o in out[3:6]),
        *out[6:9],
        *out[9:12],
    )


def solution(mesh):
    in_specs = (
        P("group", None, "dp", "tensor"),
        P(None, "dp", "tensor"),
        P(None, "dp", "tensor"),
        P("group", "dp", None),
        P("dp", None),
        P("dp", None),
        P("group", None, "dp"),
        P(None, "dp"),
        P(None, "dp"),
        P("group", "dp", "tensor"),
        P("dp", "tensor"),
        P("dp", "tensor"),
        P("tensor", None),
        P(),
    )
    out_specs = (
        P(None, "dp", "tensor"),
        P(None, "dp", "tensor"),
        P(None, "dp", "tensor"),
        P("dp", None),
        P("dp", None),
        P("dp", None),
        P(None, "dp"),
        P(None, "dp"),
        P(None, "dp"),
        P("dp", "tensor"),
        P("dp", "tensor"),
        P("dp", "tensor"),
    )
    body = functools.partial(local, mesh.shape["group"], mesh.shape["tensor"])
    return jax.shard_map(body, mesh=mesh, in_specs=in_specs, out_specs=out_specs, check_vma=False)
```

time: 242 us -> 68.6 us (0.28)
  waiting for transfers between devices: 103 us -> 0 us
  blocking collectives: 92.5 us -> 0 us
  Pallas kernels: 0 us -> 63 us
  between operations: 14.9 us -> 1.32 us
  local copies, waits for them, and re-layouts: 17.2 us -> 3.82 us
  other arithmetic: 11.9 us -> 0 us
    pallas_call x0 -> x2, Pallas kernels: none -> 63 us  [the longest x1 57.8 us: local(): pl.pallas_call(functools.partial(exchange_kernel, chips, tensors, chunks,...]
    psum x1 -> x0, blocking collectives: 60.9 us -> none  [local(): factors = lax.psum(partial_factors, ('group', 'tensor'))]
    all_gather x3 -> x0, waiting for transfers between devices: 57.7 us -> none  [the longest x1 36.2 us: local(): lax.all_gather(keyvalue_part[2], 'group', axis=1, tiled=True)]
    reduce_scatter x2 -> x0, waiting for transfers between devices: 43.7 us -> none  [the longest x1 43.7 us: local(): lax.psum_scatter(keyvalue_diff, 'group', scatter_dimension=1, tiled=True)]
    all_gather x6 -> x0, blocking collectives: 31.6 us -> none  [the longest x1 5.46 us: local(): lax.all_gather(router_part[2], 'group', axis=0, tiled=True)]
    unnamed x31 -> x10, local copies, waits for them, and re-layouts: 17.2 us -> 3.82 us
    sub x6 -> x0, other arithmetic: 11.9 us -> none  [the longest x1 6.04 us: local(): keyvalue_diff = keyvalue_anchor - keyvalue_local[0]]
  transfers between devices with their start and end apart: 6 -> 0, of which waited for: 3 -> 0; matrix products, arithmetic and copies ran while one was open for 4% -> 0% of each run, Pallas kernels for 0% -> 0%
where the time goes in v1:
time: 68.6 us; the launch traced here: 68.1 us
  Pallas kernels  63 us (92%)
  local copies, waits for them, and re-layouts  3.82 us (6%)
  between operations  1.32 us (2%)
    pallas_call x1, Pallas kernels, local(): pl.pallas_call(functools.partial(exchange_kernel, chips, tensors, chunks,...  57.8 us
    pallas_call x1, Pallas kernels, local(): pl.pallas_call(functools.partial(store_kernel, 12), out_shape=[jax.ShapeD...  5.2 us
    unnamed x10, local copies, waits for them, and re-layouts  3.82 us

profile of v1, /device:TPU:0, one launch (start us, length us, event | category | flops | bytes accessed | tf_op | source)
XLA Modules:
  0.0 68.1 jit_solution(5356593285002675935)
XLA Ops:
  1.3 0.0 copy-start
  1.3 0.8 %copy-done = f32[1,2048,8]{1,2,0:T(8,128)S(1)} copy-done((f32[1,2048,8]{1,2,0:T(8,128)S(1)}, f32[1,2048,8]{1,2,0:T(8,128)}, u32[]{:S(2)}) %copy-start) | copy-done | bytes 65560
  2.1 0.0 copy-start.1
  2.1 0.8 %copy-done.1 = f32[2048,8]{0,1:T(8,128)S(1)} copy-done((f32[2048,8]{0,1:T(8,128)S(1)}, f32[2048,8]{0,1:T(8,128)}, u32[]{:S(2)}) %copy-start.1) | copy-done | bytes 65560
  3.0 0.0 copy-start.2
  3.0 0.7 %copy-done.2 = f32[1,2,2048]{2,1,0:T(2,128)S(1)} copy-done((f32[1,2,2048]{2,1,0:T(2,128)S(1)}, f32[1,2,2048]{2,1,0:T(2,128)}, u32[]{:S(2)}) %copy-start.2) | copy-done | bytes 16408
  3.7 0.0 copy-start.3
  3.7 0.7 %copy-done.3 = f32[2,2048]{1,0:T(2,128)S(1)} copy-done((f32[2,2048]{1,0:T(2,128)S(1)}, f32[2,2048]{1,0:T(2,128)}, u32[]{:S(2)}) %copy-start.3) | copy-done | bytes 16408
  4.4 0.0 copy-start.4
  4.4 0.7 %copy-done.4 = f32[2,2048]{1,0:T(2,128)S(1)} copy-done((f32[2,2048]{1,0:T(2,128)S(1)}, f32[2,2048]{1,0:T(2,128)}, u32[]{:S(2)}) %copy-start.4) | copy-done | bytes 16408
  5.1 57.8 %exchange.1 = (f32[2,2048,256]{2,1,0:T(8,128)S(1)}, f32[2,2048,256]{2,1,0:T(8,128)S(1)}, f32[2,2048,256]{2,1,0:T(8,128)S(1)}, f32[8,2048]{1,0:T(8,128)S(1)}, f32...) custom-call(f32[1]{0:T(128)} %bitcast.13.rate_ref, ...), custom_call_target="tpu_custom_call" | custom-call | tf_op jit(solution)/shard_map/exchange/pallas_call | solution.py:350
  62.9 5.2 %store.1 = (f32[2,2048,256]{2,1,0:T(8,128)}, f32[2,2048,256]{2,1,0:T(8,128)}, f32[2,2048,256]{2,1,0:T(8,128)}, f32[8,2048]{1,0:T(8,128)}, f32[8,2048]{1,0:T(8,12...) custom-call(f32[2,2048,256]{2,1,0:T(8,128)S(1)} %get-tuple-element.3, ...), custom_call_target="tpu_custom_call" | custom-call | tf_op jit(solution)/shard_map/store/pallas_call | solution.py:361
Async XLA Ops:
  1.3 0.8 %copy-start = (f32[1,2048,8]{1,2,0:T(8,128)S(1)}, f32[1,2048,8]{1,2,0:T(8,128)}, u32[]{:S(2)}) copy-start(f32[1,2048,8]{1,2,0:T(8,128)} %param.17) | copy-start | bytes 196612
  2.1 0.8 %copy-start.1 = (f32[2048,8]{0,1:T(8,128)S(1)}, f32[2048,8]{0,1:T(8,128)}, u32[]{:S(2)}) copy-start(f32[2048,8]{0,1:T(8,128)} %param.18) | copy-start | bytes 196612
  3.0 0.7 %copy-start.2 = (f32[1,2,2048]{2,1,0:T(2,128)S(1)}, f32[1,2,2048]{2,1,0:T(2,128)}, u32[]{:S(2)}) copy-start(f32[1,2,2048]{2,1,0:T(2,128)} %param.20) | copy-start | bytes 49156
  3.7 0.7 %copy-start.3 = (f32[2,2048]{1,0:T(2,128)S(1)}, f32[2,2048]{1,0:T(2,128)}, u32[]{:S(2)}) copy-start(f32[2,2048]{1,0:T(2,128)} %ga.1) | copy-start | bytes 49156
  4.4 0.7 %copy-start.4 = (f32[2,2048]{1,0:T(2,128)S(1)}, f32[2,2048]{1,0:T(2,128)}, u32[]{:S(2)}) copy-start(f32[2,2048]{1,0:T(2,128)} %gs.1) | copy-start | bytes 49156

commit v2 on v1

--- a/solution.py
+++ b/solution.py
@@ -30,7 +30,7 @@
     r_d, r_pair, r_x, r_a, g_d, g_pair, g_x, g_a, f_d, f_pair, f_x, f_z, f_a,
     a_sem, l_sem, s_sem, small_sem,
     d_send, d_recv, x_send, x_recv, c_send, c_recv,
-    sd_send, sd_recv, sx_send, sx_recv, sc_send, sc_recv, z_send, z_recv,
+    sd_send, sd_recv, sx_send, sx_recv, sc_send, sc_recv, z_send, z_recv, go_sem, meet_sem,
 ):
     groups = 2 * chips
     me = lax.axis_index("group")
@@ -66,13 +66,14 @@
         copy.start()
 
     barrier = pltpu.get_barrier_semaphore()
-    pl.semaphore_signal(barrier, inc=1, device_id={"group": sibling}, device_id_type=MESH)
+
+    def greet(j):
+        peer = lax.rem(chip + j, chips) * 2
+        pl.semaphore_signal(barrier, inc=1, device_id={"group": peer}, device_id_type=MESH)
+
     for j in range(1, chips):
-        peer = lax.rem(chip + j, chips) * 2 + core
-        pl.semaphore_signal(barrier, inc=1, device_id={"group": peer}, device_id_type=MESH)
-    for j in range(1, tensors):
-        peer = lax.rem(lane + j, tensors)
-        pl.semaphore_signal(barrier, inc=1, device_id={"tensor": peer}, device_id_type=MESH)
+        greet(j)
+    pl.when(core == 1)(lambda: greet(0))
 
     lax.fori_loop(lead, chunks, start_loads, 0)
     for copy in small_loads[7:]:
@@ -82,7 +83,18 @@
     ]
     for copy in s_loads:
         copy.start()
-    pl.semaphore_wait(barrier, chips + tensors - 1)
+
+    @pl.when(core == 0)
+    def _():
+        pl.semaphore_wait(barrier, groups - 1)
+        pl.semaphore_signal(go_sem, inc=1, device_id={"group": sibling}, device_id_type=MESH)
+
+    @pl.when(core == 1)
+    def _():
+        pl.semaphore_wait(go_sem, 1)
+        for j in range(1, tensors):
+            peer = lax.rem(lane + j, tensors)
+            pl.semaphore_signal(barrier, inc=1, device_id={"tensor": peer}, device_id_type=MESH)
 
     def to_sibling(src, dst, send, recv):
         return pltpu.make_async_remote_copy(
@@ -217,6 +229,15 @@
             recv_sem=z_recv.at[source], device_id={"tensor": lax.rem(lane + j, tensors)},
             device_id_type=MESH,
         )
+
+    @pl.when(core == 1)
+    def _():
+        pl.semaphore_wait(barrier, tensors - 1)
+        pl.semaphore_signal(meet_sem, inc=1, device_id={"group": sibling}, device_id_type=MESH)
+
+    @pl.when(core == 0)
+    def _():
+        pl.semaphore_wait(meet_sem, 1)
 
     for i, (d, pair, x, a) in enumerate(smalls):
         for j in range(1, chips):
@@ -346,23 +367,24 @@
         dma(chunks), dma(chunks), dma(peers, chunks), dma(chips, chunks), dma(chunks), dma(chunks),
         dma(3), dma(3), dma(3, peers), dma(3, chips), dma(3), dma(3),
         dma(max(tensors - 1, 1)), dma(tensors),
+        pltpu.SemaphoreType.REGULAR, pltpu.SemaphoreType.REGULAR,
     ]
     hold = pl.pallas_call(
         functools.partial(exchange_kernel, chips, tensors, chunks, vocab),
         out_shape=[pltpu.VMEM(s, f32) for s in shapes],
-        in_specs=[pl.BlockSpec(memory_space=pltpu.SMEM)] + [pl.BlockSpec(memory_space=pl.ANY)] * 13,
+        in_specs=[pl.BlockSpec(memory_space=pltpu.SMEM)] + [pl.BlockSpec(memory_space=pltpu.HBM)] * 13,
         out_specs=[pl.BlockSpec(memory_space=pltpu.VMEM)] * 12,
         scratch_shapes=scratch,
         compiler_params=pltpu.CompilerParams(
             collective_id=0, has_side_effects=True, vmem_limit_bytes=40 * 2**20
         ),
         name="exchange",
-    )(*operands)
+    )(*[pltpu.with_memory_space_constraint(o, pltpu.HBM) if o.ndim > 1 else o for o in operands])
     out = pl.pallas_call(
         functools.partial(store_kernel, 12),
         out_shape=[jax.ShapeDtypeStruct(s, f32) for s in shapes],
         in_specs=[pl.BlockSpec(memory_space=pltpu.VMEM)] * 12,
-        out_specs=[pl.BlockSpec(memory_space=pl.ANY)] * 12,
+        out_specs=[pl.BlockSpec(memory_space=pltpu.HBM)] * 12,
         scratch_shapes=[dma(12)],
         compiler_params=pltpu.CompilerParams(vmem_limit_bytes=20 * 2**20),
         name="store",

time: 68.6 us -> 62.1 us (0.905)
  local copies, waits for them, and re-layouts: 3.82 us -> 0 us
  Pallas kernels: 63 us -> 60.6 us
    unnamed x10 -> x0, local copies, waits for them, and re-layouts: 3.82 us -> none
    pallas_call x1, Pallas kernels: 57.8 us -> 55.4 us  [local(): pl.pallas_call(functools.partial(exchange_kernel, chips, tensors, chunks,...]
where the time goes in v2:
time: 62.1 us; the launch traced here: 61.9 us
  Pallas kernels  60.6 us (98%)
  between operations  1.3 us (2%)
    pallas_call x1, Pallas kernels, local(): pl.pallas_call(functools.partial(exchange_kernel, chips, tensors, chunks,...  55.4 us
    pallas_call x1, Pallas kernels, local(): pl.pallas_call(functools.partial(store_kernel, 12), out_shape=[jax.ShapeD...  5.2 us

profile of v2, /device:TPU:0, one launch (start us, length us, event | category | flops | bytes accessed | tf_op | source)
XLA Modules:
  0.0 61.9 jit_solution(12310955131569773624)
XLA Ops:
  1.3 55.4 %exchange.1 = (f32[2,2048,256]{2,1,0:T(8,128)S(1)}, f32[2,2048,256]{2,1,0:T(8,128)S(1)}, f32[2,2048,256]{2,1,0:T(8,128)S(1)}, f32[8,2048]{1,0:T(8,128)S(1)}, f32...) custom-call(f32[1]{0:T(128)} %bitcast.13.rate_ref, ...), custom_call_target="tpu_custom_call" | custom-call | tf_op jit(solution)/shard_map/exchange/pallas_call | solution.py:372
  56.7 5.2 %store.1 = (f32[2,2048,256]{2,1,0:T(8,128)}, f32[2,2048,256]{2,1,0:T(8,128)}, f32[2,2048,256]{2,1,0:T(8,128)}, f32[8,2048]{1,0:T(8,128)}, f32[8,2048]{1,0:T(8,12...) custom-call(f32[2,2048,256]{2,1,0:T(8,128)S(1)} %get-tuple-element.3, ...), custom_call_target="tpu_custom_call" | custom-call | tf_op jit(solution)/shard_map/store/pallas_call | solution.py:383

commit v3 on v2

--- a/solution.py
+++ b/solution.py
@@ -8,6 +8,7 @@
 from jax.sharding import PartitionSpec as P
 
 MESH = pl.DeviceIdType.MESH
+SIZES = (1, 3, 5, 8, 8, 5, 2)
 
 
 def nesterov(average, state, anchor, rate):
@@ -22,7 +23,7 @@
 
 
 def exchange_kernel(
-    chips, tensors, chunks, vocab,
+    chips, tensors, sizes, vocab,
     rate_ref, kl, ka, ks, rl, ra, rs, gl, ga, gs, el, ea, es, eb,
     k_avg, k_mom, k_upd, r_avg, r_mom, r_upd, g_avg, g_mom, g_upd, e_avg, e_mom, e_upd,
     a_v, l_v, s_v, pair_v, x_v,
@@ -38,20 +39,21 @@
     other = 1 - core
     sibling = chip * 2 + other
     lane = lax.axis_index("tensor")
-    rows = a_v.shape[1] // chunks
-    half_rows = a_v.shape[1]
+    chunks = len(sizes)
+    starts = [sum(sizes[:c]) for c in range(chunks)]
 
     def load(src, dst, sem, half, c):
-        at = pl.multiple_of(c * rows, rows)
         return pltpu.make_async_copy(
-            src.at[half, pl.ds(at, rows), :], dst.at[half, pl.ds(at, rows), :], sem.at[half, c]
-        )
-
-    def start_loads(c, _):
+            src.at[half, part(c), :], dst.at[half, part(c), :], sem.at[half, c]
+        )
+
+    def part(c):
+        return pl.ds(starts[c], sizes[c])
+
+    def start_loads(c):
         for half in (other, core):
             load(ka, a_v, a_sem, half, c).start()
             load(kl, l_v, l_sem, half, c).start()
-        return 0
 
     small_loads = [
         pltpu.make_async_copy(src, dst, small_sem.at[i])
@@ -60,8 +62,9 @@
              (rs, rs_v), (gs, gs_v), (es, es_v)]
         )
     ]
-    lead = min(4, chunks)
-    lax.fori_loop(0, lead, start_loads, 0)
+    lead = min(3, chunks)
+    for c in range(lead):
+        start_loads(c)
     for copy in small_loads[:7]:
         copy.start()
 
@@ -75,7 +78,8 @@
         greet(j)
     pl.when(core == 1)(lambda: greet(0))
 
-    lax.fori_loop(lead, chunks, start_loads, 0)
+    for c in range(lead, chunks):
+        start_loads(c)
     for copy in small_loads[7:]:
         copy.start()
     s_loads = [
@@ -107,9 +111,6 @@
             src_ref=src, dst_ref=dst, send_sem=send, recv_sem=recv,
             device_id={"group": lax.rem(chip + j, chips) * 2 + core}, device_id_type=MESH,
         )
-
-    def part(c):
-        return pl.ds(pl.multiple_of(c * rows, rows), rows)
 
     def pair_copy(c):
         return to_sibling(l_v.at[other, part(c), :], pair_v.at[part(c), :], d_send.at[c], d_recv.at[c])
@@ -140,13 +141,13 @@
         for j in range(1, chips):
             chip_copy(c, j, chip).start()
 
-    def give_and_send(c, _):
-        give(c)
-        send(c - 1)
-        return 0
+    def give_and_send(first, last):
+        for c in range(first, last):
+            give(c)
+            send(c - 1)
 
     give(0)
-    lax.fori_loop(1, lead, give_and_send, 0)
+    give_and_send(1, lead)
 
     for copy in small_loads[:7]:
         copy.wait()
@@ -180,7 +181,7 @@
         for j in range(1, chips):
             to_chip(j, x.at[chip], x.at[chip], sx_send.at[i, j - 1], sx_recv.at[i, chip]).start()
 
-    lax.fori_loop(lead, chunks, give_and_send, 0)
+    give_and_send(lead, chunks)
     send(chunks - 1)
     for copy in s_loads + small_loads[7:]:
         copy.wait()
@@ -208,16 +209,14 @@
         k_mom[other, part(c), :] = momentum
         k_upd[other, part(c), :] = updated
 
-    def gather_and_accept(c, _):
-        gather(c)
-        accept(c - 1)
-        return 0
-
-    cut1 = max(lead, chunks // 2)
-    cut2 = max(cut1, (3 * chunks) // 4)
-    cut3 = max(cut2, (7 * chunks) // 8)
+    def gather_and_accept(first, last):
+        for c in range(first, last):
+            gather(c)
+            accept(c - 1)
+
+    cut1, cut2, cut3 = (min(lead + k, chunks) for k in (1, 2, 3))
     gather(0)
-    lax.fori_loop(1, cut1, gather_and_accept, 0)
+    gather_and_accept(1, cut1)
 
     def small_share(i, half):
         a = smalls[i][3]
@@ -254,7 +253,7 @@
             for j in range(1, tensors):
                 z_copy(j, lane).start()
 
-    lax.fori_loop(cut1, cut2, gather_and_accept, 0)
+    gather_and_accept(cut1, cut2)
 
     for j in range(1, tensors):
         z_copy(j, lax.rem(lane + j, tensors)).wait_recv()
@@ -276,7 +275,7 @@
             mom[:, at] = momentum
             upd[:, at] = updated
 
-    lax.fori_loop(cut2, cut3, gather_and_accept, 0)
+    gather_and_accept(cut2, cut3)
 
     small_share(2, other).wait_recv()
     turned = jnp.concatenate([f_a[0], f_a[1]], axis=0).T
@@ -289,17 +288,14 @@
     e_mom[...] = momentum
     e_upd[...] = updated
 
-    lax.fori_loop(cut3, chunks, gather_and_accept, 0)
+    gather_and_accept(cut3, chunks)
     accept(chunks - 1)
 
-    def drain(c, _):
+    for c in range(chunks):
         pair_copy(c).wait_send()
         for j in range(1, chips):
             chip_copy(c, j, chip).wait_send()
         share_copy(c, core).wait_send()
-        return 0
-
-    lax.fori_loop(0, chunks, drain, 0)
     for i, (d, pair, x, a) in enumerate(smalls):
         small_pair[i].wait_send()
         for j in range(1, chips):
@@ -324,9 +320,8 @@
     chips = groups // 2
     f32 = jnp.float32
     rows, width = ka.shape[0] * ka.shape[1] // 2, ka.shape[2]
-    chunks = 16
-    while rows % (8 * chunks):
-        chunks //= 2
+    sizes = tuple(k * rows // 32 for k in SIZES) if rows % 256 == 0 else (rows,)
+    chunks = len(sizes)
     vocab, columns = ea.shape
     rank = eb.shape[1]
     padded = -(-vocab // 128) * 128
@@ -370,7 +365,7 @@
         pltpu.SemaphoreType.REGULAR, pltpu.SemaphoreType.REGULAR,
     ]
     hold = pl.pallas_call(
-        functools.partial(exchange_kernel, chips, tensors, chunks, vocab),
+        functools.partial(exchange_kernel, chips, tensors, sizes, vocab),
         out_shape=[pltpu.VMEM(s, f32) for s in shapes],
         in_specs=[pl.BlockSpec(memory_space=pltpu.SMEM)] + [pl.BlockSpec(memory_space=pltpu.HBM)] * 13,
         out_specs=[pl.BlockSpec(memory_space=pltpu.VMEM)] * 12,

time: 62.1 us -> 61.3 us (0.987)
  Pallas kernels: 60.6 us -> 59.8 us
    pallas_call x1, Pallas kernels: 55.4 us -> 54.6 us  [local(): pl.pallas_call(functools.partial(exchange_kernel, chips, tensors, sizes,...]
where the time goes in v3:
time: 61.3 us; the launch traced here: 61.1 us
  Pallas kernels  59.8 us (98%)
  between operations  1.3 us (2%)
    pallas_call x1, Pallas kernels, local(): pl.pallas_call(functools.partial(exchange_kernel, chips, tensors, sizes,...  54.6 us
    pallas_call x1, Pallas kernels, local(): pl.pallas_call(functools.partial(store_kernel, 12), out_shape=[jax.ShapeD...  5.2 us

profile of v3, /device:TPU:0, one launch (start us, length us, event | category | flops | bytes accessed | tf_op | source)
XLA Modules:
  0.0 61.1 jit_solution(12470939163156480784)
XLA Ops:
  1.3 54.6 %exchange.1 = (f32[2,2048,256]{2,1,0:T(8,128)S(1)}, f32[2,2048,256]{2,1,0:T(8,128)S(1)}, f32[2,2048,256]{2,1,0:T(8,128)S(1)}, f32[8,2048]{1,0:T(8,128)S(1)}, f32...) custom-call(f32[1]{0:T(128)} %bitcast.13.rate_ref, ...), custom_call_target="tpu_custom_call" | custom-call | tf_op jit(solution)/shard_map/exchange/pallas_call | solution.py:367
  55.9 5.2 %store.1 = (f32[2,2048,256]{2,1,0:T(8,128)}, f32[2,2048,256]{2,1,0:T(8,128)}, f32[2,2048,256]{2,1,0:T(8,128)}, f32[8,2048]{1,0:T(8,128)}, f32[8,2048]{1,0:T(8,12...) custom-call(f32[2,2048,256]{2,1,0:T(8,128)S(1)} %get-tuple-element.3, ...), custom_call_target="tpu_custom_call" | custom-call | tf_op jit(solution)/shard_map/store/pallas_call | solution.py:378
